TPU v7x, 32 devices: a whole 2x2x4 slice. The times are simulated.
32 devices in a mesh: grp: 2 (over y), mp: 16 (over z, x, core).
Axes of the slice: x: 2, y: 2, z: 4, core: 2. Of those that a mesh axis runs over, the one named last changes fastest.
Arguments:
- query_grad: bfloat16 [64, 8192], P('grp'), parts along dimension 0, may hold values from -0.0625 to 0.0625
- query_input: bfloat16 [64, 8192], P('grp'), parts along dimension 0, may hold values from -6 to 6
- query_ids: int32 [64], P('grp'), parts along dimension 0, may hold values from 0 to 7, never falling along the last dimension, each value on 1 to 8 neighbouring positions
- train_grad: bfloat16 [256, 8192], P('grp'), parts along dimension 0, may hold values from -0.0625 to 0.0625
- train_input: bfloat16 [256, 8192], P('grp'), parts along dimension 0, may hold values from -3 to 3
- train_ids: int32 [256], P('grp'), parts along dimension 0, may hold values from 0 to 15, never falling along the last dimension, each value on 1 to 16 neighbouring positions
- output_basis: bfloat16 [8192, 8192], P(None, 'mp'), may hold values from -0.0625 to 0.0625
- input_basis: bfloat16 [8192, 8192], P(None, 'mp'), may hold values from -0.0625 to 0.0625
- eigenvalues: float32 [8192, 8192], P('mp'), may hold values from 0.05 to 5
Outputs:
- scores: float32 [16, 16], P('grp'), parts along dimension 0
There are 2 independent parts, one for each index of `grp`. A program takes and returns all parts, laid end to end along the dimension named above; an argument that names none is the same for every part. Nothing has to cross between parts.
Inputs may be any that keep to these rules, and one draw needn't show every extreme that they name: `query_ids`: each query is a run of consecutive tokens, 1 to 8 long, one of exactly 8; ids never fall. `train_ids`: each training example is a run of consecutive tokens, 1 to 16 long, one of exactly 16; ids never fall.
All inputs are finite; a program needn't handle non-finite values.
Results may differ from a plain program's by a relative error of at most 0.0049.
Values may be sent and summed in bfloat16 or wider, within the bound.
A program may use at most 256 MiB of HBM per device.

v0:
```python
import math
import jax
import jax.numpy as jnp
from jax import lax
from jax.sharding import PartitionSpec as P

QUERIES = 8
QMOST = 8
TRAIN = 16
damping_shift = 0.25


def rotate(basis, factors):
    return lax.dot_general(
        basis, factors, (((0,), (1,)), ((), ())), preferred_element_type=jnp.float32
    ).astype(jnp.bfloat16)


def query_window(query_ids):
    token_count = query_ids.shape[0]
    labels = jnp.arange(QUERIES, dtype=jnp.int32)
    starts = jnp.sum((query_ids[None, :] < labels[:, None]).astype(jnp.int32), axis=1)
    window = jnp.minimum(
        starts[:, None] + jnp.arange(QMOST, dtype=jnp.int32)[None, :], token_count - 1
    )
    live_slot = jnp.take(query_ids, window) == labels[:, None]
    return (window, live_slot)


def window_rows(columns, window):
    return jnp.transpose(jnp.take(columns, window, axis=1), (1, 2, 0))


def build_precond(left_window, right_cols, eig_cols, window):
    right_window = window_rows(right_cols, window)
    query_count = left_window.shape[0]
    group_size = math.gcd(query_count, 8)
    left_groups = left_window.reshape(
        (query_count // group_size, group_size) + left_window.shape[1:]
    )
    right_groups = right_window.reshape(
        (query_count // group_size, group_size) + right_window.shape[1:]
    )

    def one_group(operands):
        products = jnp.einsum(
            "qms,qma->qsa", operands[0], operands[1], preferred_element_type=jnp.float32
        )
        return (products / (eig_cols[None] + damping_shift)).astype(jnp.bfloat16)

    precond_groups = lax.map(one_group, (left_groups, right_groups))
    return precond_groups.reshape((query_count,) + precond_groups.shape[2:])


def on_device(
    query_grad,
    query_input,
    query_ids,
    train_grad,
    train_input,
    train_ids,
    output_basis,
    input_basis,
    eigenvalues,
):
    query_left = rotate(output_basis, query_grad)
    query_right = rotate(input_basis, query_input)
    train_left = rotate(output_basis, train_grad)
    train_right = rotate(input_basis, train_input)
    window, live_slot = query_window(query_ids)
    left_taken = window_rows(query_left, window)
    left_window = jnp.where(live_slot[:, :, None], left_taken, jnp.zeros((), jnp.bfloat16))
    right_full, train_full = (
        lax.all_gather(query_right, "mp", axis=0, tiled=True),
        lax.all_gather(train_right, "mp", axis=0, tiled=True),
    )
    precond = build_precond(left_window, right_full, eigenvalues, window)
    inner_sum = jnp.einsum("qsa,at->qst", precond, train_full, preferred_element_type=jnp.float32)
    contrib = jnp.einsum(
        "qst,st->qt", inner_sum, train_left.astype(jnp.float32), precision=lax.Precision.HIGHEST
    )
    onehot = (train_ids[:, None] == jnp.arange(TRAIN, dtype=jnp.int32)[None, :]).astype(jnp.float32)
    shares = jnp.dot(contrib, onehot, precision=lax.Precision.HIGHEST)
    return lax.psum(shares, "mp")


def solution(mesh):
    return jax.shard_map(
        on_device,
        mesh=mesh,
        in_specs=(
            P("grp", None),
            P("grp", None),
            P("grp"),
            P("grp", None),
            P("grp", None),
            P("grp"),
            P(None, "mp"),
            P(None, "mp"),
            P("mp", None),
        ),
        out_specs=P("grp", None),
        check_vma=False,
    )
```

profile of v0, /device:TPU:0, one launch (start us, length us, event | category | flops | bytes accessed | tf_op | source)
XLA Modules:
  0.0 167.1 jit_solution(38802841651659386)
XLA Ops:
  6.5 0.0 copy-start
  6.5 0.0 copy-start.1
  6.5 0.0 copy-start.3
  6.5 0.0 all-gather.2.cloned.1.call-start
  6.5 1.6 copy-done
  8.1 6.4 %convolution_convert_fusion = bf16[512,128]{1,0:T(8,128)(2,1)} fusion(bf16[8192,512]{1,0:T(8,128)(2,1)} %param.16, bf16[128,8192]{1,0:T(8,128)(2,1)S(1)} %copy-done), kind=kOutput, calls=%fused_computation.9 | convolution fusion | flops 1073807360 | bytes 10616832 | tf_op jit(solution)/shard_map/dot_general | solution.py:14
  14.5 0.0 all-gather.2.cloned.1.call-update
  14.6 0.0 copy-done.1
  14.6 0.1 convert_reduce_fusion
  14.7 0.1 compare_select_fusion
  14.8 0.1 reshape.101
  14.9 0.8 gather_fusion
  15.6 0.1 reshape.100
  15.7 0.1 iota_compare_fusion.2
  15.8 0.0 copy-done.3
  15.8 4.9 %convolution_convert_fusion.2 = bf16[512,32]{0,1:T(8,128)(2,1)S(1)} fusion(bf16[32,8192]{1,0:T(8,128)(2,1)S(1)} %copy-done.3, bf16[8192,512]{1,0:T(8,128)(2,1)} %param.16), kind=kOutput, calls=%fused_computation.13 | convolution fusion | flops 268451840 | bytes 8945664 | tf_op jit(solution)/shard_map/dot_general | solution.py:14
  20.7 24.6 %all_gather.6 = bf16[8192,32]{0,1:T(8,128)(2,1)S(1)} all-gather(bf16[512,32]{0,1:T(8,128)(2,1)S(1)} %convolution_convert_fusion.2), channel_id=1, replica_groups=mesh['grp'=2,'mp'=16] {'mp'}, dimensions={0}, use_global_device_ids=true | all-gather | bytes 557056 | tf_op jit(solution)/shard_map/all_gather | solution.py:74
  45.4 0.0 copy-start.4
  45.4 2.2 %gather_fusion.2 = bf16[64,8192]{1,0:T(8,128)(2,1)} fusion(bf16[8192,32]{0,1:T(8,128)(2,1)S(1)} %all_gather.6, s32[1024]{0:T(1024)S(1)} %pad_clamp_fusion), kind=kCustom, calls=%fused_computation.2 | custom fusion | bytes 2097408 | tf_op jit(solution)/shard_map/jit(_take)/gather | solution.py:31
  47.6 0.0 copy-done.4
  47.6 4.9 %convolution_convert_fusion.3 = bf16[512,32]{0,1:T(8,128)(2,1)S(1)} fusion(bf16[32,8192]{1,0:T(8,128)(2,1)S(1)} %copy-done.4, bf16[8192,512]{1,0:T(8,128)(2,1)} %param.15), kind=kOutput, calls=%fused_computation.14 | convolution fusion | flops 268451840 | bytes 8945664 | tf_op jit(solution)/shard_map/dot_general | solution.py:14
  52.5 0.7 gather_fusion.1
  53.2 0.0 copy-start.2
  53.2 11.9 %broadcast_add_fusion = f32[512,8192]{1,0:T(8,128)} fusion(f32[512,8192]{1,0:T(8,128)} %param.17), kind=kLoop, calls=%fused_computation.6 | loop fusion | flops 4194304 | bytes 33554432 | tf_op jit(solution)/shard_map/while/body/eval_jaxpr/add | solution.py:49
  65.1 0.0 copy-done.2
  65.1 30.2 %divide_convert_fusion.6 = bf16[8,512,8192]{2,1,0:T(8,128)(2,1)} fusion(f32[512,8192]{1,0:T(8,128)} %broadcast_add_fusion, bf16[64,8192]{1,0:T(8,128)(2,1)S(1)} %copy-done.2, pred[8,8]{1,0:T(8,128)(4,1)S(1)} %get-tuple-element.14, bf16[64,512]{1,0:T(8,128)(2,1)S(1)} %gather_fusion.1, pred[8,8]{1,0:T(8,128)(4,1)S(1)} %get-tuple-element.13), kind=kOutput, calls=%fused_computation.3.clone.clone.clone.clone.1 | convolution fusion | flops 604569600 | bytes 85000320 | tf_op jit(solution)/shard_map/while/body/eval_jaxpr/qms,qma->qsa/dot_general | solution.py:46
  95.3 6.3 %fusion.7 = f32[128,512]{0,1:T(8,128)S(1)} fusion(bf16[8192,512]{1,0:T(8,128)(2,1)} %param.15, bf16[128,8192]{1,0:T(8,128)(2,1)} %param.12), kind=kOutput, calls=%fused_computation.12 | convolution fusion | flops 1073872896 | bytes 10747904 | tf_op jit(solution)/shard_map/dot_general | solution.py:14
  101.7 0.0 copy-start.5
  101.7 0.0 all-gather.2.cloned.1.call-done
  101.7 27.9 %multiply_reduce_fusion = f32[128,8]{0,1:T(8,128)S(1)} fusion(bf16[8192,128]{1,0:T(8,128)(2,1)} %all-gather.2.cloned.1.call-done, f32[128,512]{0,1:T(8,128)S(1)} %fusion.7, bf16[8,512,8192]{2,1,0:T(8,128)(2,1)} %divide_convert_fusion.6), kind=kOutput, calls=%fused_computation.8 | convolution fusion | flops 8590982144 | bytes 69472256 | tf_op jit(solution)/shard_map/qsa,at->qst/dot_general | solution.py:78
  129.6 0.0 copy-done.5
  129.7 0.2 fusion.19
  129.8 30.4 %psum.7 = f32[8,16]{1,0:T(8,128)} all-reduce(f32[8,16]{1,0:T(8,128)S(1)} %fusion.19), channel_id=1, replica_groups=mesh['grp'=2,'mp'=16] {'mp'}, use_global_device_ids=true, to_apply=%region_1.2 | all-reduce | flops 128 | bytes 1024 | tf_op jit(solution)/shard_map/psum | solution.py:84
  (1 shorter events, 0.0 us)
Async XLA Ops:
  6.5 1.6 copy-start
  6.5 8.0 %copy-start.1 = (s32[32]{0:T(128)S(1)}, s32[32]{0:T(128)}, u32[]{:S(2)}) copy-start(s32[32]{0:T(128)} %param.11) | copy-start | bytes 388
  6.5 9.3 %copy-start.3 = (bf16[32,8192]{1,0:T(8,128)(2,1)S(1)}, bf16[32,8192]{1,0:T(8,128)(2,1)}, u32[]{:S(2)}) copy-start(bf16[32,8192]{1,0:T(8,128)(2,1)} %param.10) | copy-start | bytes 1572868
  6.5 95.2 %all-gather.2.cloned.1.call-start = ((), (), s32[]{:S(2)}) async-start(), calls=%async_computation | async-start | bytes 2228224 | tf_op jit(solution)/shard_map/all_gather | solution.py:75
  45.4 2.2 %copy-start.4 = (bf16[32,8192]{1,0:T(8,128)(2,1)S(1)}, bf16[32,8192]{1,0:T(8,128)(2,1)}, u32[]{:S(2)}) copy-start(bf16[32,8192]{1,0:T(8,128)(2,1)} %param.9) | copy-start | bytes 1572868
  53.2 11.9 %copy-start.2 = (bf16[64,8192]{1,0:T(8,128)(2,1)S(1)}, bf16[64,8192]{1,0:T(8,128)(2,1)}, u32[]{:S(2)}) copy-start(bf16[64,8192]{1,0:T(8,128)(2,1)} %gather_fusion.2) | copy-start | bytes 3145732
  101.7 28.0 %copy-start.5 = (s32[128]{0:T(128)S(1)}, s32[128]{0:T(128)}, u32[]{:S(2)}) copy-start(s32[128]{0:T(128)} %param.14) | copy-start | bytes 1540
Sparse Core Ops, SparseCore 0:
  14.7 44.4 all-gather.1
where the time goes:
time: 167 us
  matrix products  81 us (49%)
  blocking collectives  55.1 us (33%)
  between operations  13.5 us (8%)
  other arithmetic  12.1 us (7%)
  local copies, waits for them, and re-layouts  5.45 us (3%)
    psum x1, blocking collectives, on_device(): return lax.psum(shares, 'mp')  30.4 us
    dot_general x1, matrix products, one_group(): jnp.einsum('qms,qma->qsa', operands[0], operands[1], preferred_element_ty...  30.2 us
    dot_general x1, matrix products, on_device(): jnp.einsum('qsa,at->qst', precond, train_full, preferred_element_type=jnp...  27.9 us
    all_gather x1, blocking collectives, on_device(): lax.all_gather(query_right, 'mp', axis=0, tiled=True)  24.6 us
    dot_general x4, matrix products, rotate(): lax.dot_general(basis, factors, (((0,), (1,)), ((), ())), preferred_eleme...  22.6 us
    add x1, other arithmetic, one_group(): return (products / (eig_cols[None] + damping_shift)).astype(jnp.bfloat16)  11.9 us
  transfers between devices with their start and end apart: 1, of which 0 were waited for; matrix products, arithmetic and copies ran while one was open for 37% of the time, Pallas kernels for 0%

commit v1 on v0

--- a/solution.py
+++ b/solution.py
@@ -81,7 +81,7 @@
     )
     onehot = (train_ids[:, None] == jnp.arange(TRAIN, dtype=jnp.int32)[None, :]).astype(jnp.float32)
     shares = jnp.dot(contrib, onehot, precision=lax.Precision.HIGHEST)
-    return lax.psum(shares, "mp")
+    return jnp.sum(lax.all_gather(shares, "mp"), 0)
 
 
 def solution(mesh):

time: 167 us -> 155 us (0.928)
  blocking collectives: 55.1 us -> 42.3 us
    psum x1 -> x0, blocking collectives: 30.4 us -> none  [on_device(): return lax.psum(shares, 'mp')]
    all_gather x0 -> x1, blocking collectives: none -> 17.6 us  [on_device(): return jnp.sum(lax.all_gather(shares, 'mp'), 0)]
  transfers between devices with their start and end apart: 1 -> 1, of which waited for: 0 -> 0; matrix products, arithmetic and copies ran while one was open for 37% -> 40% of each run, Pallas kernels for 0% -> 0%
where the time goes in v1:
time: 155 us
  matrix products  81 us (52%)
  blocking collectives  42.3 us (27%)
  between operations  13.5 us (9%)
  other arithmetic  12.8 us (8%)
  local copies, waits for them, and re-layouts  5.45 us (4%)
    dot_general x1, matrix products, one_group(): jnp.einsum('qms,qma->qsa', operands[0], operands[1], preferred_element_ty...  30.2 us
    dot_general x1, matrix products, on_device(): jnp.einsum('qsa,at->qst', precond, train_full, preferred_element_type=jnp...  27.9 us
    all_gather x1, blocking collectives, on_device(): lax.all_gather(query_right, 'mp', axis=0, tiled=True)  24.6 us
    dot_general x4, matrix products, rotate(): lax.dot_general(basis, factors, (((0,), (1,)), ((), ())), preferred_eleme...  22.6 us
    all_gather x1, blocking collectives, on_device(): return jnp.sum(lax.all_gather(shares, 'mp'), 0)  17.6 us
    add x1, other arithmetic, one_group(): return (products / (eig_cols[None] + damping_shift)).astype(jnp.bfloat16)  11.9 us
  transfers between devices with their start and end apart: 1, of which 0 were waited for; matrix products, arithmetic and copies ran while one was open for 40% of the time, Pallas kernels for 0%

profile of v1, /device:TPU:0, one launch (start us, length us, event | category | flops | bytes accessed | tf_op | source)
XLA Modules:
  0.0 154.9 jit_solution(14958794453660524945)
XLA Ops:
  6.5 0.0 copy-start
  6.5 0.0 copy-start.1
  6.5 0.0 copy-start.3
  6.5 0.0 all-gather.3.cloned.1.call-start
  6.5 1.6 %copy-done = bf16[128,8192]{1,0:T(8,128)(2,1)S(1)} copy-done((bf16[128,8192]{1,0:T(8,128)(2,1)S(1)}, bf16[128,8192]{1,0:T(8,128)(2,1)}, u32[]{:S(2)}) %copy-start) | copy-done | bytes 2097176
  8.1 6.4 %convolution_convert_fusion = bf16[512,128]{1,0:T(8,128)(2,1)} fusion(bf16[8192,512]{1,0:T(8,128)(2,1)} %param.16, bf16[128,8192]{1,0:T(8,128)(2,1)S(1)} %copy-done), kind=kOutput, calls=%fused_computation.9 | convolution fusion | flops 1073807360 | bytes 10616832 | tf_op jit(solution)/shard_map/dot_general | solution.py:14
  14.5 0.0 all-gather.3.cloned.1.call-update
  14.6 0.0 copy-done.1
  14.6 0.1 convert_reduce_fusion
  14.7 0.1 compare_select_fusion
  14.8 0.1 reshape.101
  14.9 0.8 gather_fusion
  15.6 0.1 reshape.100
  15.7 0.1 iota_compare_fusion.2
  15.8 0.0 copy-done.3
  15.8 4.9 %convolution_convert_fusion.2 = bf16[512,32]{0,1:T(8,128)(2,1)S(1)} fusion(bf16[32,8192]{1,0:T(8,128)(2,1)S(1)} %copy-done.3, bf16[8192,512]{1,0:T(8,128)(2,1)} %param.16), kind=kOutput, calls=%fused_computation.13 | convolution fusion | flops 268451840 | bytes 8945664 | tf_op jit(solution)/shard_map/dot_general | solution.py:14
  20.7 24.6 %all_gather.12 = bf16[8192,32]{0,1:T(8,128)(2,1)S(1)} all-gather(bf16[512,32]{0,1:T(8,128)(2,1)S(1)} %convolution_convert_fusion.2), channel_id=1, replica_groups=mesh['grp'=2,'mp'=16] {'mp'}, dimensions={0}, use_global_device_ids=true | all-gather | bytes 557056 | tf_op jit(solution)/shard_map/all_gather | solution.py:74
  45.4 0.0 copy-start.4
  45.4 2.2 %gather_fusion.2 = bf16[64,8192]{1,0:T(8,128)(2,1)} fusion(bf16[8192,32]{0,1:T(8,128)(2,1)S(1)} %all_gather.12, s32[1024]{0:T(1024)S(1)} %pad_clamp_fusion), kind=kCustom, calls=%fused_computation.2 | custom fusion | bytes 2097408 | tf_op jit(solution)/shard_map/jit(_take)/gather | solution.py:31
  47.6 0.0 copy-done.4
  47.6 4.9 %convolution_convert_fusion.3 = bf16[512,32]{0,1:T(8,128)(2,1)S(1)} fusion(bf16[32,8192]{1,0:T(8,128)(2,1)S(1)} %copy-done.4, bf16[8192,512]{1,0:T(8,128)(2,1)} %param.15), kind=kOutput, calls=%fused_computation.14 | convolution fusion | flops 268451840 | bytes 8945664 | tf_op jit(solution)/shard_map/dot_general | solution.py:14
  52.5 0.7 gather_fusion.1
  53.2 0.0 copy-start.2
  53.2 11.9 %broadcast_add_fusion = f32[512,8192]{1,0:T(8,128)} fusion(f32[512,8192]{1,0:T(8,128)} %param.17), kind=kLoop, calls=%fused_computation.6 | loop fusion | flops 4194304 | bytes 33554432 | tf_op jit(solution)/shard_map/while/body/eval_jaxpr/add | solution.py:49
  65.1 0.0 copy-done.2
  65.1 30.2 %divide_convert_fusion.6 = bf16[8,512,8192]{2,1,0:T(8,128)(2,1)} fusion(f32[512,8192]{1,0:T(8,128)} %broadcast_add_fusion, bf16[64,8192]{1,0:T(8,128)(2,1)S(1)} %copy-done.2, pred[8,8]{1,0:T(8,128)(4,1)S(1)} %get-tuple-element.14, bf16[64,512]{1,0:T(8,128)(2,1)S(1)} %gather_fusion.1, pred[8,8]{1,0:T(8,128)(4,1)S(1)} %get-tuple-element.13), kind=kOutput, calls=%fused_computation.3.clone.clone.clone.clone.1 | convolution fusion | flops 604569600 | bytes 85000320 | tf_op jit(solution)/shard_map/while/body/eval_jaxpr/qms,qma->qsa/dot_general | solution.py:46
  95.3 6.3 %fusion.7 = f32[128,512]{0,1:T(8,128)S(1)} fusion(bf16[8192,512]{1,0:T(8,128)(2,1)} %param.15, bf16[128,8192]{1,0:T(8,128)(2,1)} %param.12), kind=kOutput, calls=%fused_computation.12 | convolution fusion | flops 1073872896 | bytes 10747904 | tf_op jit(solution)/shard_map/dot_general | solution.py:14
  101.7 0.0 copy-start.5
  101.7 0.0 all-gather.3.cloned.1.call-done
  101.7 27.9 %multiply_reduce_fusion = f32[128,8]{0,1:T(8,128)S(1)} fusion(bf16[8192,128]{1,0:T(8,128)(2,1)} %all-gather.3.cloned.1.call-done, f32[128,512]{0,1:T(8,128)S(1)} %fusion.7, bf16[8,512,8192]{2,1,0:T(8,128)(2,1)} %divide_convert_fusion.6), kind=kOutput, calls=%fused_computation.8 | convolution fusion | flops 8590982144 | bytes 69472256 | tf_op jit(solution)/shard_map/qsa,at->qst/dot_general | solution.py:78
  129.6 0.0 copy-done.5
  129.7 0.2 fusion.19
  129.8 17.6 %all-gather = f32[128,16]{1,0:T(8,128)S(1)} all-gather(f32[8,16]{1,0:T(8,128)S(1)} %fusion.19), channel_id=2, replica_groups=mesh['grp'=2,'mp'=16] {'mp'}, dimensions={0}, use_global_device_ids=true | all-gather | bytes 8704 | tf_op jit(solution)/shard_map/all_gather | solution.py:84
  147.5 0.6 bitcast_reduce_fusion
  (1 shorter events, 0.0 us)
Async XLA Ops:
  6.5 1.6 %copy-start = (bf16[128,8192]{1,0:T(8,128)(2,1)S(1)}, bf16[128,8192]{1,0:T(8,128)(2,1)}, u32[]{:S(2)}) copy-start(bf16[128,8192]{1,0:T(8,128)(2,1)} %param.13) | copy-start | bytes 6291460
  6.5 8.0 %copy-start.1 = (s32[32]{0:T(128)S(1)}, s32[32]{0:T(128)}, u32[]{:S(2)}) copy-start(s32[32]{0:T(128)} %param.11) | copy-start | bytes 388
  6.5 9.3 %copy-start.3 = (bf16[32,8192]{1,0:T(8,128)(2,1)S(1)}, bf16[32,8192]{1,0:T(8,128)(2,1)}, u32[]{:S(2)}) copy-start(bf16[32,8192]{1,0:T(8,128)(2,1)} %param.10) | copy-start | bytes 1572868
  6.5 95.2 %all-gather.3.cloned.1.call-start = ((), (), s32[]{:S(2)}) async-start(), calls=%async_computation | async-start | bytes 2228224 | tf_op jit(solution)/shard_map/all_gather | solution.py:75
  45.4 2.2 %copy-start.4 = (bf16[32,8192]{1,0:T(8,128)(2,1)S(1)}, bf16[32,8192]{1,0:T(8,128)(2,1)}, u32[]{:S(2)}) copy-start(bf16[32,8192]{1,0:T(8,128)(2,1)} %param.9) | copy-start | bytes 1572868
  53.2 11.9 %copy-start.2 = (bf16[64,8192]{1,0:T(8,128)(2,1)S(1)}, bf16[64,8192]{1,0:T(8,128)(2,1)}, u32[]{:S(2)}) copy-start(bf16[64,8192]{1,0:T(8,128)(2,1)} %gather_fusion.2) | copy-start | bytes 3145732
  101.7 28.0 %copy-start.5 = (s32[128]{0:T(128)S(1)}, s32[128]{0:T(128)}, u32[]{:S(2)}) copy-start(s32[128]{0:T(128)} %param.14) | copy-start | bytes 1540
Sparse Core Ops, SparseCore 0:
  14.7 44.4 all-gather.2
